TPU v7x, 32 devices: a whole 2x2x4 slice. The times are simulated.
32 devices in a mesh: det: 4 (over z), src: 8 (over y, x, core).
Axes of the slice: x: 2, y: 2, z: 4, core: 2. Of those that a mesh axis runs over, the one named last changes fastest.
Arguments:
- patches: bfloat16 [2048, 2, 128, 128], P(('det', 'src')), may hold values from -0.046875 to 0.046875
- owners: int32 [2048, 2], P(('det', 'src')), may hold values from 0 to 7, all different within a row; in each aligned block of 64 rows (0 to 63, 64 to 127, ...) at most 32 rows name the same one
- tap_weights: float32 [8, 2, 31], P('src'), may hold values from -0.1 to 1.2
Outputs:
- gram_self: float32 [2048, 512], P(('det', 'src'))
- gram_cross: float32 [2048, 512], P(('det', 'src'))
Inputs may be any that keep to these rules, and one draw needn't show every extreme that they name: `owners`: each row names 2 different source blocks. Among the 64 detectors of one device (aligned blocks of rows) no block is named more than 32 times, and in every draw some device names some block exactly 32 times.
All inputs are finite; a program needn't handle non-finite values.
Results may differ from a plain program's by a relative error of at most 0.0093.
Values may be sent and summed in bfloat16 or wider, within the bound.
A program may use at most 128 MiB of HBM per device.

v0:
```python
import jax
import jax.numpy as jnp
from jax import lax
from jax.sharding import PartitionSpec as P

exact_mode = lax.Precision.HIGHEST


def from_partner(value, axis, apart):
    return lax.ppermute(value, axis, [(i, i ^ 1 << apart) for i in range(lax.axis_size(axis))])


def build_table(block_edge, tap_count):
    offset = (
        jnp.arange(block_edge, dtype=jnp.int32)[None, :]
        - jnp.arange(block_edge, dtype=jnp.int32)[:, None]
        + tap_count // 2
    )
    return (offset[None, :, :] == jnp.arange(tap_count, dtype=jnp.int32)[:, None, None]).astype(
        jnp.float32
    )


def make_bands(tap_rows, band_table):
    return jnp.einsum("...t,tij->...ij", tap_rows, band_table, precision=exact_mode).astype(
        jnp.bfloat16
    )


def on_device(patches, owners, tap_weights):
    src_count = lax.axis_size("src")
    det_count = lax.axis_size("det")
    det_dev = patches.shape[0]
    touch_count = patches.shape[1]
    block_edge = patches.shape[2]
    records = det_dev * touch_count
    capacity = 2 * records // src_count
    slot_total = capacity * src_count
    panel_width = det_dev * src_count
    pieces = patches.reshape(records, block_edge, block_edge)
    owner_of = owners.reshape(records)
    record_ids = jnp.arange(records, dtype=jnp.int32)
    earlier_same = (owner_of[:, None] == owner_of[None, :]) & (
        record_ids[None, :] < record_ids[:, None]
    )
    position = jnp.sum(earlier_same.astype(jnp.int32), axis=1)
    slot_index = owner_of * capacity + position
    slot_match = slot_index[None, :] == jnp.arange(slot_total, dtype=jnp.int32)[:, None]
    filled = jnp.any(slot_match, axis=1)
    source = jnp.sum(jnp.where(slot_match, record_ids[None, :], 0), axis=1)
    panel_base = lax.axis_index("src") * det_dev
    slot_ids = jnp.where(filled, panel_base + source // touch_count, -1)
    band_table = build_table(block_edge, tap_weights.shape[-1])
    outgoing = jnp.where(
        filled[:, None, None], jnp.take(pieces, source, axis=0), jnp.zeros((), jnp.bfloat16)
    )
    arrived, arrived_ids = (
        lax.all_to_all(
            outgoing.reshape(src_count, capacity, block_edge, block_edge),
            "src",
            split_axis=0,
            concat_axis=0,
            tiled=True,
        ),
        lax.all_to_all(
            slot_ids.reshape(src_count, capacity), "src", split_axis=0, concat_axis=0, tiled=True
        ),
    )
    arrived = arrived.reshape(slot_total, block_edge, block_edge)
    owned_ids = arrived_ids.reshape(slot_total)
    own_bands = make_bands(tap_weights[0], band_table)
    half_owned = jnp.einsum(
        "nic,rc->nir", arrived, own_bands[0], preferred_element_type=jnp.float32
    ).astype(jnp.bfloat16)
    smoothed = jnp.einsum(
        "ki,nij->nkj", own_bands[1], half_owned, preferred_element_type=jnp.float32
    ).astype(jnp.bfloat16)
    partner, partner_ids = from_partner((smoothed, owned_ids), "det", det_count.bit_length() - 2)
    own_flat = smoothed.reshape(slot_total, block_edge * block_edge)
    other_flat = partner.reshape(slot_total, block_edge * block_edge)
    contract = (((1,), (1,)), ((), ()))
    gram_mine = lax.dot_general(own_flat, own_flat, contract, preferred_element_type=jnp.float32)
    gram_other = lax.dot_general(own_flat, other_flat, contract, preferred_element_type=jnp.float32)
    columns = jnp.arange(panel_width, dtype=jnp.int32)
    onehot_mine = (owned_ids[:, None] == columns[None, :]).astype(jnp.float32)
    onehot_other = (partner_ids[:, None] == columns[None, :]).astype(jnp.float32)
    projected = jnp.concatenate(
        [
            jnp.dot(gram_mine, onehot_mine, precision=exact_mode),
            jnp.dot(gram_other, onehot_other, precision=exact_mode),
        ],
        axis=1,
    )
    stacked = lax.psum_scatter(
        lax.dot_general(
            onehot_mine,
            projected,
            (((0,), (0,)), ((), ())),
            precision=exact_mode,
            preferred_element_type=jnp.float32,
        ),
        "src",
        scatter_dimension=0,
        tiled=True,
    )
    result_self = stacked[:, :panel_width]
    result_cross = stacked[:, panel_width:]
    return (result_self, result_cross)


def solution(mesh):
    return jax.shard_map(
        on_device,
        mesh=mesh,
        in_specs=(
            P(("det", "src"), None, None, None),
            P(("det", "src"), None),
            P("src", None, None),
        ),
        out_specs=(P(("det", "src"), None), P(("det", "src"), None)),
        check_vma=False,
    )
```

profile of v0, /device:TPU:1, one launch (start us, length us, event | category | flops | bytes accessed | tf_op | source)
XLA Modules:
  0.0 571.4 jit_solution(9876776043252830563)
XLA Ops:
  7.2 0.0 copy-start
  7.2 0.8 copy.14
  8.0 0.1 reshape.156
  8.1 0.2 convert_reduce_fusion
  8.3 0.1 select_reduce_fusion
  8.4 0.1 fusion.19
  8.5 0.1 reduce_sum.27
  8.6 0.1 broadcast_in_dim.53
  8.7 10.7 %gather_fusion = bf16[256,128,128]{2,1,0:T(8,128)(2,1)} fusion(bf16[128,128,128]{2,1,0:T(8,128)(2,1)} %bitcast.33, s32[1024]{0:T(1024)S(1)} %pad_clamp_fusion), kind=kCustom, calls=%fused_computation | custom fusion | bytes 16778240 | tf_op jit(solution)/shard_map/jit(_take)/gather | solution.py:55
  19.4 7.4 %select_select_fusion = bf16[8,32,128,128]{3,2,1,0:T(8,128)(2,1)} fusion(bf16[8,32,128,128]{3,2,1,0:T(8,128)(2,1)} %bitcast.32, pred[8,32]{1,0:T(8,128)(4,1)S(1)} %compare_and_fusion, pred[8,32]{1,0:T(8,128)(4,1)S(1)} %broadcast_in_dim.53), kind=kLoop, calls=%fused_computation.4 | loop fusion | flops 8388608 | bytes 16777728 | tf_op jit(solution)/shard_map/jit(_where)/select_n | solution.py:54
  26.8 5.2 all-to-all-start.1
  32.0 0.0 reduce-scatter.2.cloned.1.call-start
  32.0 0.0 copy-done
  32.1 0.8 fusion.8
  32.9 0.1 fusion.34
  33.0 89.6 %all-to-all-done.1 = bf16[8,32,128,128]{3,2,1,0:T(8,128)(2,1)} async-done(((bf16[8,32,128,128]{3,2,1,0:T(8,128)(2,1)}), bf16[8,32,128,128]{3,2,1,0:T(8,128)(2,1)}, u32[]{:S(2)}, u32[]{:S(2)}) %all-to-all-start.1) | async-done | bytes 8388640 | tf_op jit(solution)/shard_map/all_to_all | solution.py:58
  122.6 9.2 %convert_bitcast_fusion = bf16[256,128,128]{1,2,0:T(8,128)(2,1)} fusion(bf16[256,128,128]{2,1,0:T(8,128)(2,1)} %bitcast.5, bf16[1,128,128]{2,0,1:T(2,128)(2,1)S(1)} %get-tuple-element.5, bf16[1,128,128]{2,0,1:T(2,128)(2,1)S(1)} %get-tuple-element.4), kind=kOutput, calls=%fused_computation.1 | convolution fusion | flops 2155872256 | bytes 16842752 | tf_op jit(solution)/shard_map/ki,nij->nkj/dot_general | solution.py:75
  131.8 3.4 collective-permute-start
  135.3 0.1 reduce_sum.26
  135.3 0.1 reduce_or.12
  135.4 10.2 %all_to_all.11 = s32[8,1,32]{2,1,0:T(1,128)S(1)} all-to-all(s32[8,1,32]{2,1,0:T(1,128)S(1)} %bitcast.34), channel_id=1, replica_groups=mesh['det'=4,'src'=8] {'src'}, dimensions={0} | all-to-all | bytes 2048 | tf_op jit(solution)/shard_map/all_to_all | solution.py:65
  145.7 0.5 broadcast.128
  146.2 0.7 reduce.3
  146.9 0.1 eq.73
  147.0 0.1 collective-permute-start.1
  147.1 12.0 %copy.17 = bf16[256,128,128]{2,0,1:T(8,128)(2,1)} copy(bf16[256,128,128]{1,2,0:T(8,128)(2,1)} %convert_bitcast_fusion) | data formatting | bytes 16777216 | tf_op jit(solution)/shard_map/convert_element_type | solution.py:77
  159.1 8.1 %convolution_bitcast_fusion.1 = f32[256,256]{1,0:T(8,128)S(1)} fusion(bf16[256,128,128]{2,0,1:T(8,128)(2,1)} %copy.17), kind=kOutput, calls=%fused_computation.9 | convolution fusion | flops 2147483648 | bytes 8650752 | tf_op jit(solution)/shard_map/dot_general | solution.py:82
  167.2 0.5 fusion.14
  167.7 327.5 %collective-permute-done = bf16[256,128,128]{1,2,0:T(8,128)(2,1)} collective-permute-done((bf16[256,128,128]{1,2,0:T(8,128)(2,1)}, bf16[256,128,128]{1,2,0:T(8,128)(2,1)}, u32[]{:S(2)}, u32[]{:S(2)}) %collective-permute-start) | collective-permute-done | bytes 8388640 | tf_op jit(solution)/shard_map/ppermute | solution.py:10
  495.2 0.0 copy-start.1
  495.2 11.8 %copy.20 = bf16[256,128,128]{2,0,1:T(8,128)(2,1)} copy(bf16[256,128,128]{1,2,0:T(8,128)(2,1)} %collective-permute-done) | data formatting | bytes 16777216 | tf_op jit(solution)/shard_map/ppermute | solution.py:10
  506.9 8.1 %convolution_bitcast_fusion = f32[256,256]{1,0:T(8,128)S(1)} fusion(bf16[256,128,128]{2,0,1:T(8,128)(2,1)} %copy.17, bf16[256,128,128]{2,0,1:T(8,128)(2,1)} %copy.20), kind=kOutput, calls=%fused_computation.8 | convolution fusion | flops 2147483648 | bytes 17039360 | tf_op jit(solution)/shard_map/dot_general | solution.py:83
  515.1 0.0 collective-permute-done.1
  515.1 0.5 fusion.15
  515.6 2.5 fusion.9
  518.1 0.0 reduce-scatter.2.cloned.1.call-update
  518.1 44.8 %reduce-scatter.2.cloned.1.call-done = f32[64,1024]{1,0:T(8,128)} async-done(((f32[512,1024]{1,0:T(8,128)}), f32[64,1024]{1,0:T(8,128)}) %reduce-scatter.2.cloned.1.call-update) | async-done | bytes 262160 | tf_op jit(solution)/shard_map/reduce_scatter | solution.py:94
  562.9 1.7 fusion.33
  564.6 0.0 copy-done.1
  (6 shorter events, 0.0 us)
Async XLA Ops:
  7.2 24.9 %copy-start = (f32[1,2,31]{2,1,0:T(2,128)S(1)}, f32[1,2,31]{2,1,0:T(2,128)}, u32[]{:S(2)}) copy-start(f32[1,2,31]{2,1,0:T(2,128)} %param.5) | copy-start | bytes 748
  26.8 95.8 %all-to-all-start.1 = ((bf16[8,32,128,128]{3,2,1,0:T(8,128)(2,1)}), bf16[8,32,128,128]{3,2,1,0:T(8,128)(2,1)}, u32[]{:S(2)}, u32[]{:S(2)}) async-start(bf16[8,32,128,128]{3,2,1,0:T(8,128)(2,1)} %select_select_fusion), calls=%async_computation.1 | async-start | bytes 16777216 | tf_op jit(solution)/shard_map/all_to_all | solution.py:58
  32.0 530.8 %reduce-scatter.2.cloned.1.call-start = ((), (), s32[]{:S(2)}) async-start(), calls=%async_computation.3 | async-start | bytes 2359296 | tf_op jit(solution)/shard_map/reduce_scatter | solution.py:94
  131.8 363.3 %collective-permute-start = (bf16[256,128,128]{1,2,0:T(8,128)(2,1)}, bf16[256,128,128]{1,2,0:T(8,128)(2,1)}, u32[]{:S(2)}, u32[]{:S(2)}) collective-permute-start(bf16[256,128,128]{1,2,0:T(8,128)(2,1)} %convert_bitcast_fusion), channel_id=1, source_target_pairs={{0,16},{8,24},{16,0},{24,8},{1,17},{9,25},{17,1},{25,9},{2,18},{10... | collective-permute-start | bytes 25165832 | tf_op jit(solution)/shard_map/ppermute | solution.py:10
  147.0 368.1 %collective-permute-start.1 = (s32[256]{0:T(256)S(1)}, s32[256]{0:T(256)S(1)}, u32[]{:S(2)}, u32[]{:S(2)}) collective-permute-start(s32[256]{0:T(256)S(1)} %eq.73), channel_id=1, source_target_pairs={{0,16},{8,24},{16,0},{24,8},{1,17},{9,25},{17,1},{25,9},{2,18},{10... | collective-permute-start | bytes 3080 | tf_op jit(solution)/shard_map/ppermute | solution.py:10
  495.2 69.4 %copy-start.1 = (f32[1,2,31]{2,1,0:T(2,128)S(1)}, f32[1,2,31]{2,1,0:T(2,128)}, u32[]{:S(2)}) copy-start(f32[1,2,31]{2,1,0:T(2,128)} %param.5) | copy-start | bytes 748
Sparse Core Ops, SparseCore 0:
  518.2 44.6 reduce-scatter.1
where the time goes:
time: 573 us; the launch traced here: 571 us
  waiting for transfers between devices  462 us (81%)
  local copies, waits for them, and re-layouts  38.1 us (7%)
  matrix products  29.8 us (5%)
  between operations  14.1 us (2%)
  blocking collectives  10.2 us (2%)
  starting transfers between devices  8.8 us (2%)
  other arithmetic  8.53 us (1%)
    ppermute x2, waiting for transfers between devices, from_partner(): lax.ppermute(value, axis, [(i, i ^ 1 << apart) for i in range(lax.axis_si...  327 us
    all_to_all x1, waiting for transfers between devices, on_device(): lax.all_to_all(outgoing.reshape(src_count, capacity, block_edge, block_ed...  89.6 us
    reduce_scatter x1, waiting for transfers between devices, on_device(): lax.psum_scatter(lax.dot_general(onehot_mine, projected, (((0,), (0,)), (...  44.8 us
    convert_element_type x1, local copies, waits for them, and re-layouts, on_device(): smoothed = jnp.einsum('ki,nij->nkj', own_bands[1], half_owned, preferred_...  12 us
    ppermute x1, local copies, waits for them, and re-layouts, from_partner(): lax.ppermute(value, axis, [(i, i ^ 1 << apart) for i in range(lax.axis_si...  11.8 us
  transfers between devices with their start and end apart: 4, of which 3 were waited for; matrix products, arithmetic and copies ran while one was open for 8% of the time, Pallas kernels for 0%

commit v1 on v0

v1 whole, which is shorter than its diff:
```python
import functools

import jax
import jax.numpy as jnp
from jax import lax
from jax.experimental import pallas as pl
from jax.experimental.pallas import tpu as pltpu
from jax.sharding import PartitionSpec as P


def make_bands(taps, edge):
    count = taps.shape[-1]
    place = jnp.arange(edge, dtype=jnp.int32)
    offset = place[None, :] - place[:, None] + count // 2
    table = (offset[None] == jnp.arange(count, dtype=jnp.int32)[:, None, None]).astype(jnp.float32)
    return jnp.einsum("...t,tij->...ij", taps, table, precision=lax.Precision.HIGHEST).astype(
        jnp.bfloat16
    )


def smooth_kernel(owner_ref, patch_ref, band_ref, out_ref):
    touch, rows = out_ref.shape[0], out_ref.shape[1]
    base = pl.program_id(0) * rows

    for i in range(rows):
        for t in range(touch):
            own = owner_ref[base + i, t]
            half = lax.dot_general(
                patch_ref[i, t],
                band_ref[own, 0],
                (((1,), (1,)), ((), ())),
                preferred_element_type=jnp.float32,
            ).astype(jnp.bfloat16)
            out_ref[t, i] = jnp.dot(
                band_ref[own, 1], half, preferred_element_type=jnp.float32
            ).astype(jnp.bfloat16)


def smooth(patches, owners, bands):
    det, touch, edge, _ = patches.shape
    step = 8
    return pl.pallas_call(
        smooth_kernel,
        grid_spec=pltpu.PrefetchScalarGridSpec(
            num_scalar_prefetch=1,
            grid=(det // step,),
            in_specs=[
                pl.BlockSpec((step, touch, edge, edge), lambda g, o: (g, 0, 0, 0)),
                pl.BlockSpec(bands.shape, lambda g, o: (0, 0, 0, 0)),
            ],
            out_specs=pl.BlockSpec((touch, step, edge, edge), lambda g, o: (0, g, 0, 0)),
        ),
        out_shape=jax.ShapeDtypeStruct((touch, det, edge, edge), jnp.bfloat16),
        compiler_params=pltpu.CompilerParams(vmem_limit_bytes=32 << 20),
    )(owners, patches, bands)


def gram_kernel(left_ref, right_ref, left_own_ref, right_own_ref, out_ref):
    touch = left_ref.shape[0]
    total = None
    for t in range(touch):
        for u in range(touch):
            part = lax.dot_general(
                left_ref[t],
                right_ref[u],
                (((1,), (1,)), ((), ())),
                preferred_element_type=jnp.float32,
            )
            same = left_own_ref[:, t : t + 1] == right_own_ref[u : u + 1, :]
            part = jnp.where(same, part, 0.0)
            total = part if total is None else total + part
    out_ref[...] = total.astype(jnp.bfloat16)


def gram(left, right, left_own, right_own):
    touch, count, depth = right.shape
    block = 256
    return pl.pallas_call(
        gram_kernel,
        grid=(count // block, count // block),
        in_specs=[
            pl.BlockSpec((touch, block, depth), lambda i, j: (0, i, 0)),
            pl.BlockSpec((touch, block, depth), lambda i, j: (0, j, 0)),
            pl.BlockSpec((block, touch), lambda i, j: (i, 0)),
            pl.BlockSpec((touch, block), lambda i, j: (0, j)),
        ],
        out_specs=pl.BlockSpec((block, block), lambda i, j: (i, j)),
        out_shape=jax.ShapeDtypeStruct((count, count), jnp.bfloat16),
        compiler_params=pltpu.CompilerParams(vmem_limit_bytes=32 << 20),
        cost_estimate=pl.CostEstimate(
            flops=2 * touch * touch * count * count * depth,
            bytes_accessed=4 * touch * count * depth,
            transcendentals=0,
        ),
    )(left, right, left_own, right_own.T)


def share(parts, src):
    rows = parts.shape[0] // src
    got = lax.all_to_all(parts, "src", split_axis=0, concat_axis=0, tiled=True)
    return jnp.sum(got.reshape(src, rows, -1).astype(jnp.float32), axis=0)


def on_device(patches, owners, tap_weights):
    src = lax.axis_size("src")
    det_axis = lax.axis_size("det")
    det, touch, edge, _ = patches.shape
    cells = edge * edge
    swap = [(i, (i + det_axis // 2) % det_axis) for i in range(det_axis)]
    taps = lax.all_gather(tap_weights, "src", axis=0, tiled=True)
    panel_own = lax.all_gather(owners, "src", axis=0, tiled=True)
    other_own = lax.ppermute(panel_own, "det", swap)
    bands = make_bands(taps, edge)
    smoothed = smooth(patches, owners, bands).reshape(touch, det, cells)
    upper = lax.axis_index("det") >= det_axis // 2
    low, high = smoothed[:, :, : cells // 2], smoothed[:, :, cells // 2 :]
    kept = jnp.where(upper, high, low)
    given = jnp.where(upper, low, high)
    other = lax.ppermute(given, "det", swap)
    chunks = jnp.stack([kept.reshape(touch, det, src, -1), given.reshape(touch, det, src, -1)], 3)
    mine = lax.all_to_all(
        chunks.reshape(touch, det, cells), "src", split_axis=2, concat_axis=1, tiled=True
    )
    self_part = gram(mine, mine, panel_own, panel_own)
    result_self = share(self_part, src)
    theirs = lax.all_to_all(other, "src", split_axis=2, concat_axis=1, tiled=True)
    cross = gram(mine, theirs, panel_own, other_own)
    rows = share(cross, src)
    columns = share(cross.T, src)
    result_cross = rows + lax.ppermute(columns.astype(jnp.bfloat16), "det", swap).astype(
        jnp.float32
    )
    return result_self, result_cross


def solution(mesh):
    return jax.shard_map(
        on_device,
        mesh=mesh,
        in_specs=(
            P(("det", "src"), None, None, None),
            P(("det", "src"), None),
            P("src", None, None),
        ),
        out_specs=(P(("det", "src"), None), P(("det", "src"), None)),
        check_vma=False,
    )
```

time: 573 us -> 361 us (0.63); the launches traced: 571 us -> 354 us
  waiting for transfers between devices: 462 us -> 93.9 us
  local copies, waits for them, and re-layouts: 38.1 us -> 131 us
  blocking collectives: 10.2 us -> 52.3 us
  Pallas kernels: 0 us -> 35.1 us
  matrix products: 29.8 us -> 0.89 us
  starting transfers between devices: 8.8 us -> 22.9 us
  between operations: 14.1 us -> 0.75 us
  other arithmetic: 8.53 us -> 17.1 us
    ppermute x2 -> x3, waiting for transfers between devices: 327 us -> 90.7 us  [the longest x1 90.7 us: on_device(): other = lax.ppermute(given, 'det', swap)]
    all_to_all x1 -> x4, waiting for transfers between devices: 89.6 us -> 3.23 us  [the longest x2 3.23 us: share(): got = lax.all_to_all(parts, 'src', split_axis=0, concat_axis=0, tiled=True)]
    reduce_scatter x1 -> x0, waiting for transfers between devices: 44.8 us -> none  [on_device(): lax.psum_scatter(lax.dot_general(onehot_mine, projected, (((0,), (0,)), (...]
    unnamed x5 -> x17, local copies, waits for them, and re-layouts: 0.79 us -> 42.9 us
    all_gather x0 -> x2, blocking collectives: none -> 39.8 us  [the longest x1 29.5 us: on_device(): panel_own = lax.all_gather(owners, 'src', axis=0, tiled=True)]
    pallas_call x0 -> x3, Pallas kernels: none -> 35.1 us  [the longest x1 24.3 us: smooth(): pl.pallas_call(smooth_kernel, grid_spec=pltpu.PrefetchScalarGridSpec(num_...]
    dot_general x7 -> x1, matrix products: 29.8 us -> 0.89 us  [make_bands(): jnp.einsum('...t,tij->...ij', taps, table, precision=lax.Precision.HIGHEST)]
    all_to_all x1 -> x2, local copies, waits for them, and re-layouts: 0.51 us -> 29.3 us  [the longest x1 20.2 us: on_device(): lax.all_to_all(chunks.reshape(touch, det, cells), 'src', split_axis=2, co...]
  transfers between devices with their start and end apart: 4 -> 7, of which waited for: 3 -> 2; matrix products, arithmetic and copies ran while one was open for 8% -> 18% of each run, Pallas kernels for 0% -> 3%
where the time goes in v1:
time: 361 us; the launch traced here: 354 us
  local copies, waits for them, and re-layouts  131 us (36%)
  waiting for transfers between devices  93.9 us (26%)
  blocking collectives  52.3 us (14%)
  Pallas kernels  35.1 us (10%)
  starting transfers between devices  22.9 us (6%)
  other arithmetic  17.1 us (5%)
    ppermute x1, waiting for transfers between devices, on_device(): other = lax.ppermute(given, 'det', swap)  90.7 us
    unnamed x17, local copies, waits for them, and re-layouts  42.9 us
    all_gather x1, blocking collectives, on_device(): panel_own = lax.all_gather(owners, 'src', axis=0, tiled=True)  29.5 us
    pallas_call x1, Pallas kernels, smooth(): pl.pallas_call(smooth_kernel, grid_spec=pltpu.PrefetchScalarGridSpec(num_...  24.3 us
    reshape x1, local copies, waits for them, and re-layouts, on_device(): chunks.reshape(touch, det, cells)  21.6 us
    all_to_all x1, local copies, waits for them, and re-layouts, on_device(): lax.all_to_all(chunks.reshape(touch, det, cells), 'src', split_axis=2, co...  20.2 us
    another operation x2, local copies, waits for them, and re-layouts, on_device(): jnp.stack([kept.reshape(touch, det, src, -1), given.reshape(touch, det, s...  18.6 us
    all_to_all x1, blocking collectives, share(): got = lax.all_to_all(parts, 'src', split_axis=0, concat_axis=0, tiled=True)  12.4 us
  transfers between devices with their start and end apart: 7, of which 2 were waited for; matrix products, arithmetic and copies ran while one was open for 18% of the time, Pallas kernels for 3%

profile of v1, /device:TPU:1, one launch (start us, length us, event | category | flops | bytes accessed | tf_op | source)
XLA Modules:
  0.0 353.6 jit_solution(1519461249662430112)
XLA Ops:
  0.7 10.3 %all_gather.6 = f32[8,2,31]{2,1,0:T(2,128)S(1)} all-gather(f32[1,2,31]{2,1,0:T(2,128)} %param.5), channel_id=1, replica_groups=mesh['det'=4,'src'=8] {'src'}, dimensions={0}, use_global_device_ids=true | all-gather | bytes 2232 | tf_op jit(solution)/shard_map/all_gather | solution.py:110
  11.0 0.9 fusion.1
  11.9 0.1 copy.66
  12.0 0.8 copy.40.owner_ref
  12.8 2.2 copy-done.3
  15.0 24.3 %shard_map.50 = bf16[2,64,128,128]{3,2,1,0:T(8,128)(2,1)S(1)} custom-call(s32[64,2]{1,0:T(8,128)S(1)} %copy.40.owner_ref, bf16[64,2,128,128]{3,2,1,0:T(8,128)(2,1)S(1)} %copy-done.3, bf16[8,2,128,128]{3,2,1,0:T(8,128)(2,1)S(1)} %bitcast.41), custom_call_target="tpu_custom_call" | custom-call | tf_op jit(solution)/shard_map/pallas_call | solution.py:42
  39.3 2.0 copy-done
  41.3 7.3 %reshape.35 = bf16[2,64,16384]{2,1,0:T(8,128)(2,1)} reshape(bf16[2,64,128,128]{3,2,1,0:T(8,128)(2,1)} %copy-done) | data formatting | bytes 8388608 | tf_op jit(solution)/shard_map/reshape | solution.py:114
  48.5 3.9 %broadcast_select_fusion.1 = (bf16[2,64,8192]{2,1,0:T(8,128)(2,1)}, bf16[2,64,8192]{2,1,0:T(8,128)(2,1)S(1)}) fusion(pred[]{:T(512)S(6)} %ge.3, bf16[2,64,16384]{2,1,0:T(8,128)(2,1)} %reshape.35), kind=kLoop, calls=%fused_computation.5 | loop fusion | flops 2097152 | bytes 8388609 | tf_op jit(solution)/shard_map/jit(_where)/select_n | solution.py:117
  52.4 7.5 %stack_reshape.9 = bf16[2,64,8,1,1024]{4,3,2,1,0:T(2,128)(2,1)} reshape(bf16[2,64,8192]{2,1,0:T(8,128)(2,1)S(1)} %get-tuple-element.3) | data formatting | bytes 4194304 | tf_op jit(solution)/shard_map/stack;reshape | solution.py:120
  59.9 11.1 %stack_reshape.8 = bf16[2,64,8,1,1024]{4,3,2,1,0:T(2,128)(2,1)} reshape(bf16[2,64,8192]{2,1,0:T(8,128)(2,1)} %get-tuple-element.2) | data formatting | bytes 4194304 | tf_op jit(solution)/shard_map/stack;reshape | solution.py:120
  71.0 11.7 %pad_maximum_fusion = bf16[2,64,8,2,1024]{4,3,2,1,0:T(2,128)(2,1)} fusion(bf16[2,64,8,1,1024]{4,3,2,1,0:T(2,128)(2,1)} %stack_reshape.9, bf16[2,64,8,1,1024]{4,3,2,1,0:T(2,128)(2,1)} %stack_reshape.8), kind=kLoop, calls=%fused_computation | loop fusion | flops 8388608 | bytes 8388608 | tf_op jit(solution)/shard_map/stack | solution.py:120
  82.8 21.6 %copy.54 = bf16[2,64,8,2,1024]{1,0,4,3,2:T(2,128)(2,1)} copy(bf16[2,64,8,2,1024]{4,3,2,1,0:T(2,128)(2,1)} %pad_maximum_fusion) | data formatting | bytes 8388608 | tf_op jit(solution)/shard_map/reshape | solution.py:122
  104.3 10.5 %reshape.41 = bf16[8,2,131072]{2,1,0:T(2,128)(2,1)} reshape(bf16[16384,2,64]{2,1,0:T(2,128)(2,1)} %bitcast.44) | data formatting | bytes 8388608
  114.8 4.6 %all-to-all-start = ((bf16[8,2,131072]{2,1,0:T(2,128)(2,1)}), bf16[8,2,131072]{2,1,0:T(2,128)(2,1)}, u32[]{:S(2)}, u32[]{:S(2)}) async-start(bf16[8,2,131072]{2,1,0:T(2,128)(2,1)} %reshape.41), calls=%async_computation | async-start | bytes 8388608 | tf_op jit(solution)/shard_map/all_to_all | solution.py:121
  119.5 2.3 collective-permute-start
  121.8 90.7 %collective-permute-done = bf16[2,64,8192]{2,1,0:T(8,128)(2,1)} collective-permute-done((bf16[2,64,8192]{2,1,0:T(8,128)(2,1)S(1)}, bf16[2,64,8192]{2,1,0:T(8,128)(2,1)}, u32[]{:S(2)}, u32[]{:S(2)}) %collective-permute-start) | collective-permute-done | bytes 2097184 | tf_op jit(solution)/shard_map/ppermute | solution.py:119
  212.5 9.5 %copy.48 = bf16[2,64,8192]{1,0,2:T(2,128)(2,1)} copy(bf16[2,64,8192]{2,1,0:T(8,128)(2,1)} %collective-permute-done) | data formatting | bytes 4194304 | tf_op jit(solution)/shard_map/ppermute | solution.py:119
  222.0 7.6 %reshape.43 = bf16[8,2,65536]{2,1,0:T(2,128)(2,1)} reshape(bf16[8192,2,64]{2,1,0:T(2,128)(2,1)} %bitcast.46) | data formatting | bytes 4194304
  229.5 0.0 all-to-all-done
  229.5 4.9 %all-to-all-start.2 = ((bf16[8,2,65536]{2,1,0:T(2,128)(2,1)}), bf16[8,2,65536]{2,1,0:T(2,128)(2,1)S(1)}, u32[]{:S(2)}, u32[]{:S(2)}) async-start(bf16[8,2,65536]{2,1,0:T(2,128)(2,1)} %reshape.43), calls=%async_computation.2 | async-start | bytes 4194304 | tf_op jit(solution)/shard_map/all_to_all | solution.py:126
  234.4 0.0 copy-done.4
  234.4 29.5 %all-gather = s32[8,64,2]{1,2,0:T(2,128)S(1)} all-gather(s32[1,64,2]{1,2,0:T(2,128)S(1)} %bitcast.49), channel_id=1, replica_groups=mesh['det'=4,'src'=8] {'src'}, dimensions={0}, use_global_device_ids=true | all-gather | bytes 4608 | tf_op jit(solution)/shard_map/all_gather | solution.py:111
  263.9 0.1 reshape.38
  264.0 0.1 copy.47.left_own_ref
  264.1 10.3 %reshape.42 = bf16[16384,2,64]{2,1,0:T(2,128)(2,1)} reshape(bf16[8,2,131072]{2,1,0:T(2,128)(2,1)} %all-to-all-done) | data formatting | bytes 8388608
  274.5 20.2 %copy.56 = bf16[2,64,8,2048]{3,1,2,0:T(8,128)(2,1)} copy(bf16[2,64,8,2048]{1,0,3,2:T(2,128)(2,1)} %bitcast.45) | data formatting | bytes 8388608 | tf_op jit(solution)/shard_map/all_to_all | solution.py:121
  294.7 2.2 copy-done.1
  296.9 6.7 %shard_map.51 = bf16[512,512]{1,0:T(8,128)(2,1)} custom-call(bf16[2,512,2048]{2,1,0:T(8,128)(2,1)S(1)} %bitcast.37, bf16[2,512,2048]{2,1,0:T(8,128)(2,1)S(1)} %bitcast.38, s32[512,2]{1,0:T(8,128)S(1)} %copy.47.left_own_ref, s32[2,512]{1,0:T(2,128)S(1)} %bitcast.42), custom_call_target="tpu_custom_call" | custom-call | flops 4294967296 | bytes 8388608 | tf_op jit(solution)/shard_map/pallas_call | solution.py:78
  303.6 0.0 all-to-all-done.2
  303.6 3.6 %all-to-all-start.1 = ((bf16[8,64,512]{2,1,0:T(8,128)(2,1)}), bf16[8,64,512]{2,1,0:T(8,128)(2,1)S(1)}, u32[]{:S(2)}, u32[]{:S(2)}) async-start(bf16[8,64,512]{2,1,0:T(8,128)(2,1)} %bitcast.11), calls=%async_computation.1 | async-start | bytes 1048576 | tf_op jit(solution)/shard_map/all_to_all | solution.py:100
  307.2 0.0 collective-permute-start.1
  307.2 5.0 %reshape.44 = bf16[8192,2,64]{2,1,0:T(2,128)(2,1)} reshape(bf16[8,2,65536]{2,1,0:T(2,128)(2,1)S(1)} %all-to-all-done.2) | data formatting | bytes 4194304
  312.2 9.1 %copy.58 = bf16[2,64,8,1024]{3,1,2,0:T(8,128)(2,1)S(1)} copy(bf16[2,64,8,1024]{1,0,3,2:T(2,128)(2,1)} %bitcast.47) | data formatting | bytes 4194304 | tf_op jit(solution)/shard_map/all_to_all | solution.py:126
  321.3 0.0 collective-permute-done.1
  321.3 2.2 copy-done.2
  323.5 4.2 %shard_map.52 = bf16[512,512]{1,0:T(8,128)(2,1)} custom-call(bf16[2,512,2048]{2,1,0:T(8,128)(2,1)S(1)} %bitcast.39, bf16[2,512,1024]{2,1,0:T(8,128)(2,1)S(1)} %bitcast.40, s32[512,2]{1,0:T(8,128)S(1)} %copy.47.left_own_ref, s32[2,512]{1,0:T(2,128)S(1)} %bitcast.43), custom_call_target="tpu_custom_call" | custom-call | flops 2147483648 | bytes 4194304 | tf_op jit(solution)/shard_map/pallas_call | solution.py:78
  327.6 1.3 copy.52
  328.9 0.0 all-to-all-done.1
  328.9 12.4 %all_to_all.63 = bf16[8,64,512]{2,1,0:T(8,128)(2,1)S(1)} all-to-all(bf16[8,64,512]{2,1,0:T(8,128)(2,1)S(1)} %bitcast.48), channel_id=1, replica_groups=mesh['det'=4,'src'=8] {'src'}, dimensions={0} | all-to-all | bytes 1048576 | tf_op jit(solution)/shard_map/all_to_all | solution.py:100
  341.3 4.7 %all-to-all-start.3 = ((bf16[8,64,512]{2,1,0:T(8,128)(2,1)}), bf16[8,64,512]{2,1,0:T(8,128)(2,1)S(1)}, u32[]{:S(2)}, u32[]{:S(2)}) async-start(bf16[8,64,512]{2,1,0:T(8,128)(2,1)} %bitcast.18), calls=%async_computation.3 | async-start | bytes 1048576 | tf_op jit(solution)/shard_map/all_to_all | solution.py:100
  346.1 0.7 convert_reduce_fusion.1
  346.8 0.1 reduce_sum.32
  346.9 2.7 collective-permute-start.2
  349.6 3.2 all-to-all-done.3
  352.8 0.1 convert_reduce_fusion
  352.9 0.0 collective-permute-done.2
  352.9 0.7 convert_add_fusion
  (7 shorter events, 0.0 us)
Async XLA Ops:
  12.8 2.2 copy-start.3
  39.3 2.0 copy-start
  114.8 114.7 %all-to-all-start = ((bf16[8,2,131072]{2,1,0:T(2,128)(2,1)}), bf16[8,2,131072]{2,1,0:T(2,128)(2,1)}, u32[]{:S(2)}, u32[]{:S(2)}) async-start(bf16[8,2,131072]{2,1,0:T(2,128)(2,1)} %reshape.41), calls=%async_computation | async-start | bytes 8388608 | tf_op jit(solution)/shard_map/all_to_all | solution.py:121
  119.5 93.0 %collective-permute-start = (bf16[2,64,8192]{2,1,0:T(8,128)(2,1)S(1)}, bf16[2,64,8192]{2,1,0:T(8,128)(2,1)}, u32[]{:S(2)}, u32[]{:S(2)}) collective-permute-start(bf16[2,64,8192]{2,1,0:T(8,128)(2,1)S(1)} %get-tuple-element.3), channel_id=1, source_target_pairs={{0,16},{8,24},{16,0},{24,8},{1,17},{9,25},{17,1},{25,9},{2,18},{10... | collective-permute-start | bytes 6291464 | tf_op jit(solution)/shard_map/ppermute | solution.py:119
  222.0 12.5 %copy-start.4 = (s32[64,2]{0,1:T(2,128)S(1)}, s32[64,2]{0,1:T(2,128)}, u32[]{:S(2)}) copy-start(s32[64,2]{0,1:T(2,128)} %param.4) | copy-start | bytes 1540
  229.5 74.0 %all-to-all-start.2 = ((bf16[8,2,65536]{2,1,0:T(2,128)(2,1)}), bf16[8,2,65536]{2,1,0:T(2,128)(2,1)S(1)}, u32[]{:S(2)}, u32[]{:S(2)}) async-start(bf16[8,2,65536]{2,1,0:T(2,128)(2,1)} %reshape.43), calls=%async_computation.2 | async-start | bytes 4194304 | tf_op jit(solution)/shard_map/all_to_all | solution.py:126
  294.7 2.2 copy-start.1
  303.6 25.3 %all-to-all-start.1 = ((bf16[8,64,512]{2,1,0:T(8,128)(2,1)}), bf16[8,64,512]{2,1,0:T(8,128)(2,1)S(1)}, u32[]{:S(2)}, u32[]{:S(2)}) async-start(bf16[8,64,512]{2,1,0:T(8,128)(2,1)} %bitcast.11), calls=%async_computation.1 | async-start | bytes 1048576 | tf_op jit(solution)/shard_map/all_to_all | solution.py:100
  307.2 14.1 %collective-permute-start.1 = (s32[512,2]{0,1:T(2,128)S(1)}, s32[512,2]{0,1:T(2,128)S(1)}, u32[]{:S(2)}, u32[]{:S(2)}) collective-permute-start(s32[512,2]{0,1:T(2,128)S(1)} %reshape.38), channel_id=1, source_target_pairs={{0,16},{8,24},{16,0},{24,8},{1,17},{9,25},{17,1},{25,9},{2,18},{10... | collective-permute-start | bytes 12296 | tf_op jit(solution)/shard_map/ppermute | solution.py:112
  321.3 2.2 copy-start.2
  341.3 11.5 %all-to-all-start.3 = ((bf16[8,64,512]{2,1,0:T(8,128)(2,1)}), bf16[8,64,512]{2,1,0:T(8,128)(2,1)S(1)}, u32[]{:S(2)}, u32[]{:S(2)}) async-start(bf16[8,64,512]{2,1,0:T(8,128)(2,1)} %bitcast.18), calls=%async_computation.3 | async-start | bytes 1048576 | tf_op jit(solution)/shard_map/all_to_all | solution.py:100
  346.9 6.0 %collective-permute-start.2 = (bf16[64,512]{1,0:T(8,128)(2,1)S(1)}, bf16[64,512]{1,0:T(8,128)(2,1)S(1)}, u32[]{:S(2)}, u32[]{:S(2)}) collective-permute-start(bf16[64,512]{1,0:T(8,128)(2,1)S(1)} %reduce_sum.32), channel_id=1, source_target_pairs={{0,16},{8,24},{16,0},{24,8},{1,17},{9,25},{17,1},{25,9},{2,18},{10... | collective-permute-start | bytes 196616 | tf_op jit(solution)/shard_map/ppermute | solution.py:130

commit v2 on v1

v2 whole, which is shorter than its diff:
```python
import functools

import jax
import jax.numpy as jnp
from jax import lax
from jax.experimental import pallas as pl
from jax.experimental.pallas import tpu as pltpu
from jax.sharding import PartitionSpec as P

MESH = pl.DeviceIdType.MESH


def make_bands(taps, edge):
    count = taps.shape[-1]
    place = jnp.arange(edge, dtype=jnp.int32)
    offset = place[None, :] - place[:, None] + count // 2
    table = (offset[None] == jnp.arange(count, dtype=jnp.int32)[:, None, None]).astype(jnp.float32)
    return jnp.einsum("...t,tij->...ij", taps, table, precision=lax.Precision.HIGHEST).astype(
        jnp.bfloat16
    )


def smooth_kernel(owner_ref, patch_ref, band_ref, out_ref, spread_ref):
    rows, edge = patch_ref.shape[0], patch_ref.shape[2]
    t, base = pl.program_id(0), pl.program_id(1) * rows
    for i in range(rows):
        own = owner_ref[base + i, t]
        half = lax.dot_general(
            patch_ref[i, 0],
            band_ref[own, 0],
            (((1,), (1,)), ((), ())),
            preferred_element_type=jnp.float32,
        ).astype(jnp.bfloat16)
        spread_ref[pl.ds(i, edge, stride=rows), :] = jnp.dot(
            band_ref[own, 1], half, preferred_element_type=jnp.float32
        )
    out_ref[...] = spread_ref[...].reshape(out_ref.shape).astype(jnp.bfloat16)


def smooth(patches, owners, bands):
    det, touch, edge, _ = patches.shape
    step = 16
    steps = det // step
    return pl.pallas_call(
        smooth_kernel,
        grid_spec=pltpu.PrefetchScalarGridSpec(
            num_scalar_prefetch=1,
            grid=(touch, steps),
            in_specs=[
                pl.BlockSpec((step, 1, edge, edge), lambda t, g, o: (g, t, 0, 0)),
                pl.BlockSpec(bands.shape, lambda t, g, o: (0, 0, 0, 0)),
            ],
            out_specs=pl.BlockSpec((edge, step, edge), lambda t, g, o: (0, t * steps + g, 0)),
            scratch_shapes=[pltpu.VMEM((edge * step, edge), jnp.float32)],
        ),
        out_shape=jax.ShapeDtypeStruct((edge, touch * det, edge), jnp.bfloat16),
        compiler_params=pltpu.CompilerParams(vmem_limit_bytes=32 << 20),
    )(owners, patches, bands)


def gram_kernel(
    src, dets, touch, group,
    s_ref, po_ref, pot_ref, oo_ref, oot_ref,
    self_ref, cross_ref,
    mine, theirs, out_a, out_b, in_self, in_row, in_col, col_out, col_in,
    x_send, x_recv, m_send, m_recv, g_send, g_recv, c_sem,
):
    me, pd = lax.axis_index("src"), lax.axis_index("det")
    partner = lax.rem(pd + dets // 2, dets)
    upper, other_upper = pd // (dets // 2), partner // (dets // 2)
    share = mine.shape[1]
    half = share // 2
    det = mine.shape[2] // touch
    panel = src * det

    barrier = pltpu.get_barrier_semaphore()

    @pl.loop(1, src)
    def _(o):
        to = lax.rem(me + o, src)
        pl.semaphore_signal(barrier, inc=1, device_id=(pd, to), device_id_type=MESH)

    @pl.loop(0, src)
    def _(o):
        to = lax.rem(me + o, src)
        pl.semaphore_signal(barrier, inc=1, device_id=(partner, to), device_id_type=MESH)

    pl.semaphore_wait(barrier, 2 * src - 1)

    def cross_copy(o):
        to = lax.rem(me + o, src)
        return pltpu.make_async_remote_copy(
            src_ref=s_ref.at[pl.ds(to * share + other_upper * half, half)],
            dst_ref=theirs.at[me],
            send_sem=x_send.at[o],
            recv_sem=x_recv.at[o],
            device_id=(partner, to),
            device_id_type=MESH,
        )

    def self_copy(o):
        to = lax.rem(me + o, src)
        return pltpu.make_async_remote_copy(
            src_ref=s_ref.at[pl.ds(to * share, share)],
            dst_ref=mine.at[me],
            send_sem=m_send.at[o],
            recv_sem=m_recv.at[o],
            device_id=(pd, to),
            device_id_type=MESH,
        )

    def gram_copy(kind, o, source, target):
        to = lax.rem(me + o, src)
        return pltpu.make_async_remote_copy(
            src_ref=source.at[to],
            dst_ref=target.at[me],
            send_sem=g_send.at[kind, o],
            recv_sem=g_recv.at[kind, o],
            device_id=(pd, to),
            device_id_type=MESH,
        )

    def piece(ref, start, count, first, depth, t):
        return jnp.concatenate(
            [
                ref[pl.ds(start, count), first + k, t * det : (t + 1) * det, :].reshape(
                    count * det, ref.shape[3]
                )
                for k in range(depth)
            ],
            axis=1,
        )

    def partial(left, left_at, left_own, right, right_at, right_own, depth, out):
        @pl.loop(0, src // group)
        def _(g):
            start = pl.multiple_of(g * (group * det), group * det)
            total = None
            for u in range(touch):
                wide = piece(right, 0, src, right_at, depth, u)
                for t in range(touch):
                    part = lax.dot_general(
                        piece(left, g * group, group, left_at, depth, t),
                        wide,
                        (((1,), (1,)), ((), ())),
                        preferred_element_type=jnp.float32,
                    )
                    same = (
                        left_own[pl.ds(start, group * det), t : t + 1] == right_own[u : u + 1, :]
                    )
                    part = jnp.where(same, part, 0.0)
                    total = part if total is None else total + part
            out[pl.ds(g * group, group)] = total.reshape(group, det, panel).astype(jnp.bfloat16)

    def scatter(kind, source, target):
        @pl.loop(1, src)
        def _(o):
            gram_copy(kind, o, source, target).start()

        target[me] = source[me]

    def collect(kind, source, target):
        @pl.loop(1, src)
        def _(o):
            gram_copy(kind, o, source, target).wait_recv()

        total = target[0].astype(jnp.float32)
        for i in range(1, src):
            total = total + target[i].astype(jnp.float32)
        return total

    def sent(kind, source, target):
        @pl.loop(1, src)
        def _(o):
            gram_copy(kind, o, source, target).wait_send()

    @pl.loop(0, src)
    def _(o):
        cross_copy(o).start()

    own = pltpu.make_async_copy(s_ref.at[pl.ds(me * share, share)], mine.at[me], m_send.at[0])
    own.start()

    @pl.loop(1, src)
    def _(o):
        self_copy(o).start()

    own.wait()

    @pl.loop(1, src)
    def _(o):
        self_copy(o).wait()

    partial(mine, 0, po_ref, mine, 0, pot_ref, share, out_a)
    scatter(0, out_a, in_self)
    self_ref[...] = collect(0, out_a, in_self)
    sent(0, out_a, in_self)

    @pl.loop(0, src)
    def _(o):
        cross_copy(o).wait()

    partial(theirs, 0, oo_ref, mine, upper * half, pot_ref, half, out_a)
    scatter(1, out_a, in_col)
    partial(mine, upper * half, po_ref, theirs, 0, oot_ref, half, out_b)
    scatter(2, out_b, in_row)
    col_out[...] = collect(1, out_a, in_col).astype(jnp.bfloat16)
    last = pltpu.make_async_remote_copy(
        src_ref=col_out,
        dst_ref=col_in,
        send_sem=c_sem.at[0],
        recv_sem=c_sem.at[1],
        device_id=(partner, me),
        device_id_type=MESH,
    )
    last.start()
    rows = collect(2, out_b, in_row)
    sent(1, out_a, in_col)
    sent(2, out_b, in_row)
    last.wait()
    cross_ref[...] = rows + col_in[...].astype(jnp.float32)


def on_device(patches, owners, tap_weights):
    src = lax.axis_size("src")
    dets = lax.axis_size("det")
    det, touch, edge, _ = patches.shape
    panel = det * src
    share = edge // src
    swap = [(i, (i + dets // 2) % dets) for i in range(dets)]
    taps = lax.all_gather(tap_weights, "src", axis=0, tiled=True)
    panel_own = lax.all_gather(owners, "src", axis=0, tiled=True)
    other_own = lax.ppermute(panel_own, "det", swap)
    bands = make_bands(taps, edge)
    smoothed = smooth(patches, owners, bands)
    vmem = pl.BlockSpec(memory_space=pltpu.VMEM)
    dma = pltpu.SemaphoreType.DMA
    block = pltpu.VMEM((src, det, panel), jnp.bfloat16)
    line = pltpu.VMEM((det, panel), jnp.bfloat16)
    return pl.pallas_call(
        functools.partial(gram_kernel, src, dets, touch, min(src, 4)),
        out_shape=[jax.ShapeDtypeStruct((det, panel), jnp.float32)] * 2,
        in_specs=[pl.BlockSpec(memory_space=pl.ANY)] + [vmem] * 4,
        out_specs=[vmem] * 2,
        scratch_shapes=[
            pltpu.VMEM((src, share, touch * det, edge), jnp.bfloat16),
            pltpu.VMEM((src, share // 2, touch * det, edge), jnp.bfloat16),
            block, block, block, block, block, line, line,
            dma((src,)), dma((src,)), dma((src,)), dma((src,)),
            dma((3, src)), dma((3, src)), dma((2,)),
        ],
        compiler_params=pltpu.CompilerParams(
            collective_id=0, has_side_effects=True, vmem_limit_bytes=60 << 20
        ),
        cost_estimate=pl.CostEstimate(
            flops=8 * panel * panel * share * edge * 2,
            bytes_accessed=4 * det * touch * edge * edge,
            transcendentals=0,
        ),
    )(smoothed, panel_own, panel_own.T, other_own, other_own.T)


def solution(mesh):
    return jax.shard_map(
        on_device,
        mesh=mesh,
        in_specs=(
            P(("det", "src"), None, None, None),
            P(("det", "src"), None),
            P("src", None, None),
        ),
        out_specs=(P(("det", "src"), None), P(("det", "src"), None)),
        check_vma=False,
    )
```

time: 361 us -> 172 us (0.48); the launches traced: 354 us -> 172 us
  local copies, waits for them, and re-layouts: 131 us -> 9.97 us
  Pallas kernels: 35.1 us -> 139 us
  waiting for transfers between devices: 93.9 us -> 0.01 us
  blocking collectives: 52.3 us -> 19.4 us
  starting transfers between devices: 22.9 us -> 2.31 us
  other arithmetic: 17.1 us -> 0.01 us
    pallas_call x2 -> x1, Pallas kernels: 10.9 us -> 113 us  [on_device(): pl.pallas_call(functools.partial(gram_kernel, src, dets, touch, min(src,...]
    ppermute x2 -> x0, waiting for transfers between devices: 90.7 us -> none  [the longest x1 90.7 us: on_device(): other = lax.ppermute(given, 'det', swap)]
    unnamed x17 -> x13, local copies, waits for them, and re-layouts: 42.9 us -> 8.95 us
    all_to_all x2 -> x0, local copies, waits for them, and re-layouts: 29.3 us -> none  [the longest x1 20.2 us: on_device(): lax.all_to_all(chunks.reshape(touch, det, cells), 'src', split_axis=2, co...]
    reshape x2 -> x0, local copies, waits for them, and re-layouts: 28.9 us -> none  [the longest x1 21.6 us: on_device(): chunks.reshape(touch, det, cells)]
    all_gather x1, blocking collectives: 29.5 us -> 10.3 us  [on_device(): panel_own = lax.all_gather(owners, 'src', axis=0, tiled=True)]
    another operation x2 -> x0, local copies, waits for them, and re-layouts: 18.6 us -> none  [on_device(): jnp.stack([kept.reshape(touch, det, src, -1), given.reshape(touch, det, s...]
    all_to_all x4 -> x0, starting transfers between devices: 17.8 us -> none  [the longest x2 8.31 us: share(): got = lax.all_to_all(parts, 'src', split_axis=0, concat_axis=0, tiled=True)]
  transfers between devices with their start and end apart: 7 -> 1, of which waited for: 2 -> 0; matrix products, arithmetic and copies ran while one was open for 18% -> 2% of each run, Pallas kernels for 3% -> 15%
where the time goes in v2:
time: 172 us
  Pallas kernels  139 us (81%)
  blocking collectives  19.4 us (11%)
  local copies, waits for them, and re-layouts  9.97 us (6%)
  starting transfers between devices  2.31 us (1%)
    pallas_call x1, Pallas kernels, on_device(): pl.pallas_call(functools.partial(gram_kernel, src, dets, touch, min(src,...  113 us
    pallas_call x1, Pallas kernels, smooth(): pl.pallas_call(smooth_kernel, grid_spec=pltpu.PrefetchScalarGridSpec(num_...  25.6 us
    all_gather x1, blocking collectives, on_device(): panel_own = lax.all_gather(owners, 'src', axis=0, tiled=True)  10.3 us
    all_gather x1, blocking collectives, on_device(): taps = lax.all_gather(tap_weights, 'src', axis=0, tiled=True)  9.02 us
    unnamed x13, local copies, waits for them, and re-layouts  8.95 us
  transfers between devices with their start and end apart: 1, of which 0 were waited for; matrix products, arithmetic and copies ran while one was open for 2% of the time, Pallas kernels for 15%

profile of v2, /device:TPU:1, one launch (start us, length us, event | category | flops | bytes accessed | tf_op | source)
XLA Modules:
  0.0 171.9 jit_solution(8634089466949097077)
XLA Ops:
  0.6 10.3 %all-gather = s32[8,64,2]{1,2,0:T(2,128)S(1)} all-gather(s32[1,64,2]{1,2,0:T(2,128)} %bitcast.19), channel_id=1, replica_groups=mesh['det'=4,'src'=8] {'src'}, dimensions={0}, use_global_device_ids=true | all-gather | bytes 4608 | tf_op jit(solution)/shard_map/all_gather | solution.py:232
  11.0 0.1 reshape.18
  11.1 0.0 copy-start.2
  11.1 2.3 %collective-permute-start = (s32[512,2]{0,1:T(2,128)S(1)}, s32[512,2]{0,1:T(2,128)S(1)}, u32[]{:S(2)}, u32[]{:S(2)}) collective-permute-start(s32[512,2]{0,1:T(2,128)S(1)} %reshape.18), channel_id=1, source_target_pairs={{0,16},{8,24},{16,0},{24,8},{1,17},{9,25},{17,1},{25,9},{2,18},{10... | collective-permute-start | bytes 12296 | tf_op jit(solution)/shard_map/ppermute | solution.py:233
  13.4 9.0 %all_gather.6 = f32[8,2,31]{2,1,0:T(2,128)S(1)} all-gather(f32[1,2,31]{2,1,0:T(2,128)} %param.5), channel_id=1, replica_groups=mesh['det'=4,'src'=8] {'src'}, dimensions={0}, use_global_device_ids=true | all-gather | bytes 2232 | tf_op jit(solution)/shard_map/all_gather | solution.py:231
  22.4 0.9 fusion.1
  23.3 0.8 copy.13.owner_ref
  24.1 0.9 copy.15.po_ref
  24.9 0.1 copy.25
  25.1 0.0 copy-start
  25.1 2.2 %copy-done = bf16[64,2,128,128]{3,2,1,0:T(8,128)(2,1)S(1)} copy-done((bf16[64,2,128,128]{3,2,1,0:T(8,128)(2,1)S(1)}, bf16[64,2,128,128]{3,2,1,0:T(8,128)(2,1)}, u32[]{:S(2)}) %copy-start) | copy-done | bytes 4194328
  27.3 25.6 %shard_map.50.s_ref = bf16[128,128,128]{2,1,0:T(8,128)(2,1)S(1)} custom-call(s32[64,2]{1,0:T(8,128)S(1)} %copy.13.owner_ref, bf16[64,2,128,128]{3,2,1,0:T(8,128)(2,1)S(1)} %copy-done, bf16[8,2,128,128]{3,2,1,0:T(8,128)(2,1)S(1)} %bitcast.16), custom_call_target="tpu_custom_call" | custom-call | tf_op jit(solution)/shard_map/pallas_call | solution.py:44
  52.9 0.0 copy-done.2
  52.9 0.0 copy-start.1
  52.9 1.9 %copy-done.1 = bf16[128,128,128]{2,1,0:T(8,128)(2,1)} copy-done((bf16[128,128,128]{2,1,0:T(8,128)(2,1)}, bf16[128,128,128]{2,1,0:T(8,128)(2,1)S(1)}, u32[]{:S(2)}) %copy-start.1) | copy-done | bytes 4194328
  54.8 0.0 collective-permute-done
  54.8 0.0 copy-start.3
  54.8 0.9 copy.16.oo_ref
  55.7 0.0 copy-done.3
  55.7 113.1 %shard_map.51 = (f32[64,512]{1,0:T(8,128)}, f32[64,512]{1,0:T(8,128)}) custom-call(bf16[128,128,128]{2,1,0:T(8,128)(2,1)} %copy-done.1, s32[512,2]{1,0:T(8,128)} %copy.15.po_ref, s32[2,512]{1,0:T(2,128)} %bitcast.17, s32[512,2]{1,0:T(8,128)} %copy.16.oo_ref, s32[2,512]{1,0:T(2,128)} %bitcast.18), custom_call_target="tpu_custom_call" | custom-call | flops 8589934592 | bytes 8388608 | tf_op jit(solution)/shard_map/pallas_call | solution.py:240
  168.8 1.6 copy.28
  170.4 1.6 copy.29
  (2 shorter events, 0.0 us)
Async XLA Ops:
  11.1 41.8 %copy-start.2 = (s32[512,2]{0,1:T(2,128)}, s32[512,2]{0,1:T(2,128)S(1)}, u32[]{:S(2)}) copy-start(s32[512,2]{0,1:T(2,128)S(1)} %reshape.18) | copy-start | bytes 12292
  11.1 43.8 %collective-permute-start = (s32[512,2]{0,1:T(2,128)S(1)}, s32[512,2]{0,1:T(2,128)S(1)}, u32[]{:S(2)}, u32[]{:S(2)}) collective-permute-start(s32[512,2]{0,1:T(2,128)S(1)} %reshape.18), channel_id=1, source_target_pairs={{0,16},{8,24},{16,0},{24,8},{1,17},{9,25},{17,1},{25,9},{2,18},{10... | collective-permute-start | bytes 12296 | tf_op jit(solution)/shard_map/ppermute | solution.py:233
  25.1 2.2 %copy-start = (bf16[64,2,128,128]{3,2,1,0:T(8,128)(2,1)S(1)}, bf16[64,2,128,128]{3,2,1,0:T(8,128)(2,1)}, u32[]{:S(2)}) copy-start(bf16[64,2,128,128]{3,2,1,0:T(8,128)(2,1)} %patch_ref.1) | copy-start | bytes 12582916
  52.9 1.9 %copy-start.1 = (bf16[128,128,128]{2,1,0:T(8,128)(2,1)}, bf16[128,128,128]{2,1,0:T(8,128)(2,1)S(1)}, u32[]{:S(2)}) copy-start(bf16[128,128,128]{2,1,0:T(8,128)(2,1)S(1)} %shard_map.50.s_ref) | copy-start | bytes 12582916
  54.8 0.9 copy-start.3

commit v3 on v2

--- a/solution.py
+++ b/solution.py
@@ -20,49 +20,89 @@
     )
 
 
-def smooth_kernel(owner_ref, patch_ref, band_ref, out_ref, spread_ref):
-    rows, edge = patch_ref.shape[0], patch_ref.shape[2]
-    t, base = pl.program_id(0), pl.program_id(1) * rows
-    for i in range(rows):
-        own = owner_ref[base + i, t]
-        half = lax.dot_general(
-            patch_ref[i, 0],
-            band_ref[own, 0],
-            (((1,), (1,)), ((), ())),
-            preferred_element_type=jnp.float32,
-        ).astype(jnp.bfloat16)
-        spread_ref[pl.ds(i, edge, stride=rows), :] = jnp.dot(
-            band_ref[own, 1], half, preferred_element_type=jnp.float32
-        )
-    out_ref[...] = spread_ref[...].reshape(out_ref.shape).astype(jnp.bfloat16)
-
-
-def smooth(patches, owners, bands):
-    det, touch, edge, _ = patches.shape
-    step = 16
-    steps = det // step
+def spread_kernel(
+    src, dets, own_ref, tap_ref, mine_ref, other_ref, taps_ref,
+    mine, other, taps, m_send, m_recv, o_send, o_recv, t_send, t_recv,
+):
+    me, pd = lax.axis_index("src"), lax.axis_index("det")
+    partner = lax.rem(pd + dets // 2, dets)
+    barrier = pltpu.get_barrier_semaphore()
+
+    @pl.loop(1, src)
+    def _(o):
+        to = lax.rem(me + o, src)
+        pl.semaphore_signal(barrier, inc=1, device_id=(pd, to), device_id_type=MESH)
+
+    @pl.loop(0, src)
+    def _(o):
+        to = lax.rem(me + o, src)
+        pl.semaphore_signal(barrier, inc=1, device_id=(partner, to), device_id_type=MESH)
+
+    pl.semaphore_wait(barrier, 2 * src - 1)
+
+    def copy(o, source, target, send, recv, panel):
+        return pltpu.make_async_remote_copy(
+            src_ref=source,
+            dst_ref=target.at[me],
+            send_sem=send.at[o],
+            recv_sem=recv.at[o],
+            device_id=(panel, lax.rem(me + o, src)),
+            device_id_type=MESH,
+        )
+
+    @pl.loop(1, src)
+    def _(o):
+        copy(o, tap_ref, taps, t_send, t_recv, pd).start()
+        copy(o, own_ref, mine, m_send, m_recv, pd).start()
+
+    @pl.loop(0, src)
+    def _(o):
+        copy(o, own_ref, other, o_send, o_recv, partner).start()
+
+    taps[me] = tap_ref[...]
+    mine[me] = own_ref[...]
+
+    @pl.loop(1, src)
+    def _(o):
+        copy(o, tap_ref, taps, t_send, t_recv, pd).wait()
+        copy(o, own_ref, mine, m_send, m_recv, pd).wait()
+
+    @pl.loop(0, src)
+    def _(o):
+        copy(o, own_ref, other, o_send, o_recv, partner).wait()
+
+    taps_ref[...] = taps[...]
+    mine_ref[...] = mine[...]
+    other_ref[...] = other[...]
+
+
+def spread(owners, tap_weights, src, dets):
+    vmem = pl.BlockSpec(memory_space=pltpu.VMEM)
+    own = (src, *owners.shape)
+    tap = (src, *tap_weights.shape)
     return pl.pallas_call(
-        smooth_kernel,
-        grid_spec=pltpu.PrefetchScalarGridSpec(
-            num_scalar_prefetch=1,
-            grid=(touch, steps),
-            in_specs=[
-                pl.BlockSpec((step, 1, edge, edge), lambda t, g, o: (g, t, 0, 0)),
-                pl.BlockSpec(bands.shape, lambda t, g, o: (0, 0, 0, 0)),
-            ],
-            out_specs=pl.BlockSpec((edge, step, edge), lambda t, g, o: (0, t * steps + g, 0)),
-            scratch_shapes=[pltpu.VMEM((edge * step, edge), jnp.float32)],
+        functools.partial(spread_kernel, src, dets),
+        out_shape=[
+            jax.ShapeDtypeStruct(own, jnp.int32),
+            jax.ShapeDtypeStruct(own, jnp.int32),
+            jax.ShapeDtypeStruct(tap, jnp.float32),
+        ],
+        in_specs=[vmem] * 2,
+        out_specs=[vmem] * 3,
+        scratch_shapes=[
+            pltpu.VMEM(own, jnp.int32), pltpu.VMEM(own, jnp.int32), pltpu.VMEM(tap, jnp.float32),
+        ] + [pltpu.SemaphoreType.DMA((src,))] * 6,
+        compiler_params=pltpu.CompilerParams(
+            collective_id=1, has_side_effects=True, vmem_limit_bytes=16 << 20
         ),
-        out_shape=jax.ShapeDtypeStruct((edge, touch * det, edge), jnp.bfloat16),
-        compiler_params=pltpu.CompilerParams(vmem_limit_bytes=32 << 20),
-    )(owners, patches, bands)
+    )(owners, tap_weights)
 
 
 def gram_kernel(
-    src, dets, touch, group,
-    s_ref, po_ref, pot_ref, oo_ref, oot_ref,
+    src, dets, touch, group, step,
+    owner_ref, patch_ref, band_ref, po_ref, pot_ref, oo_ref, oot_ref,
     self_ref, cross_ref,
-    mine, theirs, out_a, out_b, in_self, in_row, in_col, col_out, col_in,
+    s_ref, spread_ref, mine, theirs, out_a, out_b, in_self, in_row, in_col, col_out, col_in,
     x_send, x_recv, m_send, m_recv, g_send, g_recv, c_sem,
 ):
     me, pd = lax.axis_index("src"), lax.axis_index("det")
@@ -87,22 +127,24 @@
 
     pl.semaphore_wait(barrier, 2 * src - 1)
 
-    def cross_copy(o):
-        to = lax.rem(me + o, src)
+    def cross_copy(o, first=0, count=touch * det):
+        to = lax.rem(me + o, src)
+        records = pl.ds(first, count)
         return pltpu.make_async_remote_copy(
-            src_ref=s_ref.at[pl.ds(to * share + other_upper * half, half)],
-            dst_ref=theirs.at[me],
+            src_ref=s_ref.at[pl.ds(to * share + other_upper * half, half), records],
+            dst_ref=theirs.at[me, :, records],
             send_sem=x_send.at[o],
             recv_sem=x_recv.at[o],
             device_id=(partner, to),
             device_id_type=MESH,
         )
 
-    def self_copy(o):
-        to = lax.rem(me + o, src)
+    def self_copy(o, first=0, count=touch * det):
+        to = lax.rem(me + o, src)
+        records = pl.ds(first, count)
         return pltpu.make_async_remote_copy(
-            src_ref=s_ref.at[pl.ds(to * share, share)],
-            dst_ref=mine.at[me],
+            src_ref=s_ref.at[pl.ds(to * share, share), records],
+            dst_ref=mine.at[me, :, records],
             send_sem=m_send.at[o],
             recv_sem=m_recv.at[o],
             device_id=(pd, to),
@@ -174,17 +216,40 @@
         def _(o):
             gram_copy(kind, o, source, target).wait_send()
 
-    @pl.loop(0, src)
-    def _(o):
-        cross_copy(o).start()
+    edge = patch_ref.shape[2]
+    steps = det // step
+
+    @pl.loop(0, touch * steps)
+    def _(q):
+        t, base = q // steps, lax.rem(q, steps) * step
+        for i in range(step):
+            named = owner_ref[base + i, t]
+            middle = lax.dot_general(
+                patch_ref[base + i, t],
+                band_ref[named, 0],
+                (((1,), (1,)), ((), ())),
+                preferred_element_type=jnp.float32,
+            ).astype(jnp.bfloat16)
+            spread_ref[pl.ds(i, edge, stride=step), :] = jnp.dot(
+                band_ref[named, 1], middle, preferred_element_type=jnp.float32
+            )
+        first = pl.multiple_of(q * step, step)
+        s_ref[:, pl.ds(first, step), :] = (
+            spread_ref[...].reshape(edge, step, edge).astype(jnp.bfloat16)
+        )
+
+        @pl.loop(0, src)
+        def _(o):
+            cross_copy(o, first, step).start()
+
+        @pl.when(lax.rem(q, steps) == steps - 1)
+        def _():
+            @pl.loop(1, src)
+            def _(o):
+                self_copy(o, pl.multiple_of(t * det, det), det).start()
 
     own = pltpu.make_async_copy(s_ref.at[pl.ds(me * share, share)], mine.at[me], m_send.at[0])
     own.start()
-
-    @pl.loop(1, src)
-    def _(o):
-        self_copy(o).start()
-
     own.wait()
 
     @pl.loop(1, src)
@@ -202,6 +267,10 @@
 
     partial(theirs, 0, oo_ref, mine, upper * half, pot_ref, half, out_a)
     scatter(1, out_a, in_col)
+    single = out_b.shape[0] < src
+    if single:
+        sent(1, out_a, in_col)
+        out_b = out_a
     partial(mine, upper * half, po_ref, theirs, 0, oot_ref, half, out_b)
     scatter(2, out_b, in_row)
     col_out[...] = collect(1, out_a, in_col).astype(jnp.bfloat16)
@@ -215,7 +284,8 @@
     )
     last.start()
     rows = collect(2, out_b, in_row)
-    sent(1, out_a, in_col)
+    if not single:
+        sent(1, out_a, in_col)
     sent(2, out_b, in_row)
     last.wait()
     cross_ref[...] = rows + col_in[...].astype(jnp.float32)
@@ -227,25 +297,26 @@
     det, touch, edge, _ = patches.shape
     panel = det * src
     share = edge // src
-    swap = [(i, (i + dets // 2) % dets) for i in range(dets)]
-    taps = lax.all_gather(tap_weights, "src", axis=0, tiled=True)
-    panel_own = lax.all_gather(owners, "src", axis=0, tiled=True)
-    other_own = lax.ppermute(panel_own, "det", swap)
-    bands = make_bands(taps, edge)
-    smoothed = smooth(patches, owners, bands)
+    panel_own, other_own, taps = spread(owners, tap_weights, src, dets)
+    panel_own = panel_own.reshape(panel, touch)
+    other_own = other_own.reshape(panel, touch)
+    bands = make_bands(taps.reshape(src, 2, -1), edge)
     vmem = pl.BlockSpec(memory_space=pltpu.VMEM)
     dma = pltpu.SemaphoreType.DMA
     block = pltpu.VMEM((src, det, panel), jnp.bfloat16)
     line = pltpu.VMEM((det, panel), jnp.bfloat16)
+    second = block if panel <= 1024 else pltpu.VMEM((1, det, panel), jnp.bfloat16)
     return pl.pallas_call(
-        functools.partial(gram_kernel, src, dets, touch, min(src, 4)),
+        functools.partial(gram_kernel, src, dets, touch, max(1, min(src, 32 // src)), 16),
         out_shape=[jax.ShapeDtypeStruct((det, panel), jnp.float32)] * 2,
-        in_specs=[pl.BlockSpec(memory_space=pl.ANY)] + [vmem] * 4,
+        in_specs=[pl.BlockSpec(memory_space=pltpu.SMEM)] + [vmem] * 6,
         out_specs=[vmem] * 2,
         scratch_shapes=[
+            pltpu.VMEM((edge, touch * det, edge), jnp.bfloat16),
+            pltpu.VMEM((edge * 16, edge), jnp.float32),
             pltpu.VMEM((src, share, touch * det, edge), jnp.bfloat16),
             pltpu.VMEM((src, share // 2, touch * det, edge), jnp.bfloat16),
-            block, block, block, block, block, line, line,
+            block, second, block, block, block, line, line,
             dma((src,)), dma((src,)), dma((src,)), dma((src,)),
             dma((3, src)), dma((3, src)), dma((2,)),
         ],
@@ -257,7 +328,7 @@
             bytes_accessed=4 * det * touch * edge * edge,
             transcendentals=0,
         ),
-    )(smoothed, panel_own, panel_own.T, other_own, other_own.T)
+    )(owners, patches, bands, panel_own, panel_own.T, other_own, other_own.T)
 
 
 def solution(mesh):

time: 172 us -> 146 us (0.85)
  blocking collectives: 19.4 us -> 0 us
  local copies, waits for them, and re-layouts: 9.97 us -> 6.9 us
  starting transfers between devices: 2.31 us -> 0 us
  Pallas kernels: 139 us -> 137 us
    all_gather x2 -> x0, blocking collectives: 19.4 us -> none  [the longest x1 10.3 us: on_device(): panel_own = lax.all_gather(owners, 'src', axis=0, tiled=True)]
    unnamed x13 -> x11, local copies, waits for them, and re-layouts: 8.95 us -> 4.59 us
    ppermute x1 -> x0, starting transfers between devices: 2.31 us -> none  [on_device(): other_own = lax.ppermute(panel_own, 'det', swap)]
  transfers between devices with their start and end apart: 1 -> 0, of which waited for: 0 -> 0; matrix products, arithmetic and copies ran while one was open for 2% -> 0% of each run, Pallas kernels for 15% -> 0%
where the time goes in v3:
time: 146 us; the launch traced here: 145 us
  Pallas kernels  137 us (94%)
  local copies, waits for them, and re-layouts  6.9 us (5%)
    pallas_call x1, Pallas kernels, on_device(): pl.pallas_call(functools.partial(gram_kernel, src, dets, touch, max(1, mi...  119 us
    pallas_call x1, Pallas kernels, spread(): pl.pallas_call(functools.partial(spread_kernel, src, dets), out_shape=[ja...  18.6 us
    unnamed x11, local copies, waits for them, and re-layouts  4.59 us

profile of v3, /device:TPU:1, one launch (start us, length us, event | category | flops | bytes accessed | tf_op | source)
XLA Modules:
  0.0 145.5 jit_solution(17853112092491977675)
XLA Ops:
  0.6 0.8 copy.10.own_ref.owner_ref
  1.4 0.0 copy-start.2
  1.4 0.0 copy-start.3
  1.4 0.7 copy-done.3
  2.1 18.6 %shard_map.50 = (s32[8,64,2]{2,1,0:T(8,128)S(1)}, s32[8,64,2]{2,1,0:T(8,128)S(1)}, f32[8,1,2,31]{3,2,1,0:T(2,128)S(1)}) custom-call(s32[64,2]{1,0:T(8,128)S(1)} %copy.10.own_ref.owner_ref, f32[1,2,31]{2,1,0:T(2,128)S(1)} %copy-done.3), custom_call_target="tpu_custom_call" | custom-call | tf_op jit(solution)/shard_map/pallas_call | solution.py:83
  20.7 0.0 copy-start
  20.7 0.0 copy-start.1
  20.7 0.8 fusion.1
  21.5 0.9 copy.21.band_ref
  22.4 0.7 copy.16
  23.1 0.7 copy.17
  23.8 0.0 copy-done.2
  23.8 0.0 copy-done
  23.8 0.0 copy-done.1
  23.8 118.5 %shard_map.51 = (f32[64,512]{1,0:T(8,128)}, f32[64,512]{1,0:T(8,128)}) custom-call(s32[64,2]{1,0:T(8,128)} %copy-done.2, bf16[64,2,128,128]{3,2,1,0:T(8,128)(2,1)} %patch_ref.1, bf16[8,2,128,128]{3,2,1,0:T(8,128)(2,1)} %copy.21.band_ref, s32[512,2]{1,0:T(8,128)} %bitcast.11, s32[2,512]{1,0:T(2,128)} %bitcast.15, s32[512,2]{1,0:T(8,128)} %bitcast.13, ...), custom_call_target="tpu_custom_call" | custom-call | flops 8589934592 | bytes 8388608 | tf_op jit(solution)/shard_map/pallas_call | solution.py:309
  142.3 1.6 %copy.24 = f32[64,512]{1,0:T(8,128)} copy(f32[64,512]{1,0:T(8,128)} %get-tuple-element.10) | data formatting | bytes 262144
  143.9 1.6 %copy.25 = f32[64,512]{1,0:T(8,128)} copy(f32[64,512]{1,0:T(8,128)} %get-tuple-element.11) | data formatting | bytes 262144
  (1 shorter events, 0.0 us)
Async XLA Ops:
  1.4 22.4 %copy-start.2 = (s32[64,2]{1,0:T(8,128)}, s32[64,2]{1,0:T(8,128)S(1)}, u32[]{:S(2)}) copy-start(s32[64,2]{1,0:T(8,128)S(1)} %copy.10.own_ref.owner_ref) | copy-start | bytes 1540
  1.4 0.7 copy-start.3
  20.7 3.1 %copy-start = (s32[8,64,2]{2,1,0:T(8,128)}, s32[8,64,2]{2,1,0:T(8,128)S(1)}, u32[]{:S(2)}) copy-start(s32[8,64,2]{2,1,0:T(8,128)S(1)} %get-tuple-element.6) | copy-start | bytes 12292
  20.7 3.1 %copy-start.1 = (s32[8,64,2]{2,1,0:T(8,128)}, s32[8,64,2]{2,1,0:T(8,128)S(1)}, u32[]{:S(2)}) copy-start(s32[8,64,2]{2,1,0:T(8,128)S(1)} %get-tuple-element.7) | copy-start | bytes 12292

commit v4 on v3

--- a/solution.py
+++ b/solution.py
@@ -297,9 +297,9 @@
     det, touch, edge, _ = patches.shape
     panel = det * src
     share = edge // src
-    panel_own, other_own, taps = spread(owners, tap_weights, src, dets)
-    panel_own = panel_own.reshape(panel, touch)
-    other_own = other_own.reshape(panel, touch)
+    panel_own, other_own, taps = spread(owners.T, tap_weights, src, dets)
+    panel_own = panel_own.transpose(1, 0, 2).reshape(touch, panel)
+    other_own = other_own.transpose(1, 0, 2).reshape(touch, panel)
     bands = make_bands(taps.reshape(src, 2, -1), edge)
     vmem = pl.BlockSpec(memory_space=pltpu.VMEM)
     dma = pltpu.SemaphoreType.DMA
@@ -328,7 +328,7 @@
             bytes_accessed=4 * det * touch * edge * edge,
             transcendentals=0,
         ),
-    )(owners, patches, bands, panel_own, panel_own.T, other_own, other_own.T)
+    )(owners, patches, bands, panel_own.T, panel_own, other_own.T, other_own)
 
 
 def solution(mesh):

time: 146 us -> 137 us (0.938)
  Pallas kernels: 137 us -> 127 us
  local copies, waits for them, and re-layouts: 6.9 us -> 8.65 us
    pallas_call x1, Pallas kernels: 18.6 us -> 8.3 us  [spread(): pl.pallas_call(functools.partial(spread_kernel, src, dets), out_shape=[ja...]
    transpose x0 -> x4, local copies, waits for them, and re-layouts: none -> 1.71 us  [the longest x2 1.71 us: on_device(): return pl.pallas_call(functools.partial(gram_kernel, src, dets, touch, ma...]
where the time goes in v4:
time: 137 us
  Pallas kernels  127 us (93%)
  local copies, waits for them, and re-layouts  8.65 us (6%)
    pallas_call x1, Pallas kernels, on_device(): pl.pallas_call(functools.partial(gram_kernel, src, dets, touch, max(1, mi...  119 us
    pallas_call x1, Pallas kernels, spread(): pl.pallas_call(functools.partial(spread_kernel, src, dets), out_shape=[ja...  8.3 us
    unnamed x11, local copies, waits for them, and re-layouts  5.88 us

profile of v4, /device:TPU:1, one launch (start us, length us, event | category | flops | bytes accessed | tf_op | source)
XLA Modules:
  0.0 137.0 jit_solution(7462963523533596132)
XLA Ops:
  0.6 1.4 %copy.9.owner_ref = s32[64,2]{1,0:T(8,128)} copy(s32[64,2]{0,1:T(2,128)} %param.4) | data formatting | bytes 1024 | tf_op args[1]
  2.0 0.0 copy-start
  2.0 0.7 copy-done
  2.7 0.0 copy-start.1
  2.7 0.7 copy-done.1
  3.4 8.3 %shard_map.50 = (s32[8,2,64]{2,1,0:T(2,128)S(1)}, s32[8,2,64]{2,1,0:T(2,128)S(1)}, f32[8,1,2,31]{3,2,1,0:T(2,128)S(1)}) custom-call(s32[2,64]{1,0:T(2,128)S(1)} %bitcast.13, f32[1,2,31]{2,1,0:T(2,128)S(1)} %copy-done.1), custom_call_target="tpu_custom_call" | custom-call | tf_op jit(solution)/shard_map/pallas_call | solution.py:83
  11.7 0.8 fusion.1
  12.5 0.9 copy.18.band_ref
  13.4 0.1 reshape.27.pot_ref
  13.4 0.0 copy-start.2
  13.5 0.8 copy.10.po_ref
  14.3 0.1 reshape.28.oot_ref
  14.4 0.0 copy-start.3
  14.4 0.9 copy.11.oo_ref
  15.2 0.0 copy-done.2
  15.2 0.0 copy-done.3
  15.2 118.6 %shard_map.51 = (f32[64,512]{1,0:T(8,128)}, f32[64,512]{1,0:T(8,128)}) custom-call(s32[64,2]{1,0:T(8,128)} %copy.9.owner_ref, bf16[64,2,128,128]{3,2,1,0:T(8,128)(2,1)} %patch_ref.1, bf16[8,2,128,128]{3,2,1,0:T(8,128)(2,1)} %copy.18.band_ref, s32[512,2]{1,0:T(8,128)} %copy.10.po_ref, s32[2,512]{1,0:T(2,128)} %copy-done.2, s32[512,2]{1,0:T(8,128)} %copy.11.oo_ref, ...), custom_call_target="tpu_custom_call" | custom-call | flops 8589934592 | bytes 8388608 | tf_op jit(solution)/shard_map/pallas_call | solution.py:309
  133.9 1.6 %copy.21 = f32[64,512]{1,0:T(8,128)} copy(f32[64,512]{1,0:T(8,128)} %get-tuple-element.10) | data formatting | bytes 262144
  135.4 1.6 %copy.22 = f32[64,512]{1,0:T(8,128)} copy(f32[64,512]{1,0:T(8,128)} %get-tuple-element.11) | data formatting | bytes 262144
  (3 shorter events, 0.0 us)
Async XLA Ops:
  2.0 0.7 copy-start
  2.7 0.7 copy-start.1
  13.4 1.8 %copy-start.2 = (s32[2,512]{1,0:T(2,128)}, s32[2,512]{1,0:T(2,128)S(1)}, u32[]{:S(2)}) copy-start(s32[2,512]{1,0:T(2,128)S(1)} %reshape.27.pot_ref) | copy-start | bytes 12292
  14.4 0.9 copy-start.3
